TPU v7x, 32 devices: a whole 2x2x4 slice. The times are simulated.
32 devices in a mesh: seq: 8 (over y, x, core), head: 4 (over z).
Axes of the slice: x: 2, y: 2, z: 4, core: 2. Of those that a mesh axis runs over, the one named last changes fastest.
Arguments:
- teacher_queries: bfloat16 [2048, 8192], P('seq', 'head'), may hold values from -16 to 16, as said below
- student_queries: bfloat16 [2048, 4096], P('seq', 'head'), may hold values from -16 to 16, as said below
- token_counts: int32 [8], replicated, may hold values from 1 to 256, 1536 in all
Outputs:
- student_grad: float32 [2048, 4096], P('seq', 'head')
- loss: float32 [], replicated
Inputs may be any that keep to these rules, and one draw needn't show every extreme that they name: `teacher_queries`: query entries are real values of order one; the entries of a row may share a scale. `student_queries`: query entries are real values of order one; the entries of a row may share a scale. `token_counts`: the counts sum to 1536; the largest equals 256.
All inputs are finite; a program needn't handle non-finite values.
Results may differ from a plain program's by a relative error of at most 0.0035.
Values may be sent and summed in bfloat16 or wider, within the bound.
No kernel may reach another device: no remote copies, remote signals or barrier semaphores. Data moves between devices by JAX's collectives and lax.ppermute only.
A program may use at most 64 MiB of HBM per device.

v0:
```python
import functools
import math

import jax
import jax.numpy as jnp
from jax import lax
from jax.experimental import pallas as pl
from jax.experimental.pallas import tpu as pltpu
from jax.sharding import PartitionSpec as P

DT = 8192
DS = 4096
H_REL = 128
TEACHER_DIM = DT // H_REL
STUDENT_DIM = DS // H_REL

NEGATIVE = -1e30
LOG2E = math.log2(math.e)
TEACHER_SCALE = LOG2E * TEACHER_DIM**-0.5
STUDENT_SCALE = LOG2E * STUDENT_DIM**-0.5
PAD = 8
LANES = 128
TAIL = 16
DEPTH = 256
SAFE_NORM = 320.0


def split_high_low(values):
    high = values.astype(jnp.bfloat16)
    low = (values - high.astype(jnp.float32)).astype(jnp.bfloat16)
    return high, low


def split_three(values):
    high = values.astype(jnp.bfloat16)
    rest = values - high.astype(jnp.float32)
    return (high,) + split_high_low(rest)


def at_columns(index, count, width, act):
    if width % LANES == 0:
        act(pl.ds(pl.multiple_of(index * width, LANES), width))
    else:
        for part in range(count):
            pl.when(index == part)(functools.partial(act, pl.ds(part * width, width)))


def pack_folded_kernel(blocks, chunks, me_ref, teacher_ref, student_ref, *refs):
    sends, student, sems = refs[:-2], refs[-2], refs[-1]
    rows = teacher_ref.shape[0]
    half = rows // 2

    def block(chunk, k):
        if chunk == 0:
            return sends[k]
        return sends[blocks + 2 * (chunk - 1) + k % 2].at[k // 2]

    copies = [pltpu.make_async_copy(student_ref, student, sems.at[chunks * blocks])]
    for chunk in range(chunks):
        for k in range(blocks):
            to = jnp.bitwise_xor(me_ref[0], k)
            at = pl.multiple_of((to * chunks + chunk) * LANES, LANES)
            copies.append(
                pltpu.make_async_copy(
                    teacher_ref.at[:, pl.ds(at, LANES)],
                    block(chunk, k).at[pl.ds(0, rows)],
                    sems.at[chunk * blocks + k],
                )
            )
    for copy in copies:
        copy.start()
    copies[0].wait()
    for k in range(blocks):
        to = jnp.bitwise_xor(me_ref[0], k)
        lanes = pl.ds(pl.multiple_of(to * LANES, LANES), LANES)
        top, bottom = student[:half, lanes], student[half:, lanes]
        for chunk in range(chunks):
            part = slice(chunk * (LANES // 2), (chunk + 1) * (LANES // 2))
            block(chunk, k)[rows:, :] = jnp.concatenate([top[:, part], bottom[:, part]], axis=1)
    for copy in copies[1:]:
        copy.wait()


def pack_plain_kernel(blocks, me_ref, teacher_ref, student_ref, *sends):
    teacher_width = teacher_ref.shape[1] // blocks
    student_width = student_ref.shape[1] // blocks
    for core in range(2):
        for k in range(blocks // 2):
            to = jnp.bitwise_xor(me_ref[0], 2 * k + core)

            def put_teacher(columns, send=sends[core], k=k):
                send[k, :, :teacher_width] = teacher_ref[:, columns]

            def put_student(columns, send=sends[core], k=k):
                send[k, :, teacher_width:] = student_ref[:, columns]

            at_columns(to, blocks, teacher_width, put_teacher)
            at_columns(to, blocks, student_width, put_student)


def pair_sum(parts):
    while len(parts) > 1:
        parts = [a + b for a, b in zip(parts[::2], parts[1::2])]
    return parts[0]


def tail_rows(value, width):
    thirds = [part.astype(jnp.float32) for part in split_three(value)]
    line = lax.broadcasted_iota(jnp.int32, (TAIL, width), 0)
    tail = jnp.where(line == 0, thirds[0], 0.0)
    tail = jnp.where(line == 1, thirds[1], tail)
    return jnp.where(line == 2, thirds[2], tail).astype(jnp.bfloat16)


def merge_kernel(chips, kept_ref, swapped_ref, *refs):
    kls, sends = refs[: 1 - chips], refs[1 - chips :]
    rows = kept_ref.shape[1]
    tail = tail_rows(pair_sum([kl[...] for kl in kls]), kept_ref.shape[2]) if kls else None
    for k, send in enumerate(sends):
        send[0, :rows, :] = kept_ref[k + 1]
        send[1, :rows, :] = swapped_ref[k + 1]
        if kls:
            send[0, rows:, :] = tail
            send[1, rows:, :] = tail


def arrived(refs):
    return [refs[0].at[0], refs[1].at[0]] + [ref.at[core] for ref in refs[2:] for core in range(2)]


def unpack_kernel(n_kl, me_ref, *refs):
    kls, returned, (grad_ref, loss_ref) = refs[:n_kl], refs[n_kl:-2], refs[-2:]
    rows = grad_ref.shape[0]
    blocks = arrived(returned)
    for k, block in enumerate(blocks):

        def put(columns, block=block):
            grad_ref[:, columns] = block[:rows, :].astype(jnp.float32)

        at_columns(jnp.bitwise_xor(me_ref[0], k), len(blocks), block.shape[1], put)
    own = tail_rows(pair_sum([kl[...] for kl in kls]), kls[0].shape[1])
    tails = [own] + [ref[0, rows:, :] for ref in returned[2:]]
    loss_ref[...] = pair_sum(
        [jnp.sum(tail.astype(jnp.float32), axis=0, keepdims=True) for tail in tails]
    )


def fold(values):
    rows, columns = values.shape
    return jnp.sum(values.reshape(rows // 8, 8, columns), axis=0)


def relation_kernel(folded, heads, tiles, order, n_in, n_done, last, me_ref, counts_ref, *refs):
    if order:
        sources = [refs[order.index(k)] for k in range(n_in)]
    else:
        sources = arrived(refs[:n_in])
    done = refs[n_in : n_in + 3 * n_done]
    rest = list(refs[n_in + 3 * n_done :])
    out, rest = rest[:3], rest[3:]
    pack, key_op, row_op, student_col, student_pad, teacher_prob, student_prob, weights_ref = rest[:8]
    if last:
        row_grad, key_grad, kl_sum, grad_rows = rest[8:]
    else:
        row_grad, key_grad, kl_sum = out
    f32, bf16 = jnp.float32, jnp.bfloat16
    blocks = len(sources)
    rows = teacher_prob.shape[2]
    half = rows // 2
    live = tiles * rows
    window = rows + PAD
    student_at = heads * TEACHER_DIM
    student_width = heads * STUDENT_DIM
    filled = 2 * TEACHER_DIM + 2 * STUDENT_DIM

    position = lax.broadcasted_iota(jnp.int32, (window, rows), 0)
    token = lax.broadcasted_iota(jnp.int32, (window, rows), 1)
    pack[...] = jnp.zeros(pack.shape, f32)
    places = []
    for k in range(blocks):
        owner = jnp.bitwise_xor(me_ref[0], k)
        start = sum(jnp.where(b < owner, counts_ref[b], 0) for b in range(blocks))
        base = pl.multiple_of(start // PAD * PAD, PAD)
        places.append((base, start - base, counts_ref[owner]))
    for source, (base, shift, count) in zip(sources, places):
        place = ((position == token + shift) & (token < count)).astype(bf16)
        here = pl.ds(base, window)
        if folded:
            moved = jnp.dot(place, source[:rows, :], preferred_element_type=f32)
            pack[here, :student_at] = pack[here, :student_at] + moved
            student = source[rows:, :]
            moved = jnp.dot(
                place[:, :half], student[:, :student_width], preferred_element_type=f32
            ) + jnp.dot(place[:, half:], student[:, student_width:], preferred_element_type=f32)
            pack[here, student_at:] = pack[here, student_at:] + moved
        else:
            moved = jnp.dot(place, source[...], preferred_element_type=f32)
            pack[here, :] = pack[here, :] + moved

    ones = jnp.ones((rows, DEPTH - filled), bf16)
    spare = lax.broadcasted_iota(jnp.int32, (DEPTH - filled, rows), 0)
    teacher_gap = jnp.zeros((2 * STUDENT_DIM, rows), bf16)
    student_gap = jnp.zeros((2 * TEACHER_DIM, rows), bf16)
    lane_head = lax.broadcasted_iota(jnp.int32, (rows, student_width), 1) // STUDENT_DIM
    norms = []

    def shift_rows(norm):
        parts = [part.astype(f32) for part in split_three(-norm)]
        out = jnp.where(spare == 0, parts[0], 0.0)
        out = jnp.where(spare == 1, parts[1], out)
        return jnp.where(spare == 2, parts[2], out).astype(bf16)

    for i in range(tiles):
        here = pl.ds(i * rows, rows)
        tile = pack[here, :]
        tile_t = tile.T
        tile_b = tile.astype(bf16)
        tile_s = tile[:, student_at:]
        for h in range(heads):
            tb = tile_b[:, h * TEACHER_DIM : (h + 1) * TEACHER_DIM]
            at = student_at + h * STUDENT_DIM
            sb = tile_b[:, at : at + STUDENT_DIM]
            key_op[h, here, :] = jnp.concatenate([tb, tb, sb, sb, ones], axis=1)
            teacher_t = tile_t[h * TEACHER_DIM : (h + 1) * TEACHER_DIM, :]
            student_t = tile_t[at : at + STUDENT_DIM, :]
            student_col[h, :, here] = student_t.astype(bf16)
            student_pad[h, here, :] = jnp.where(lane_head == h, tile_s, 0.0).astype(bf16)
            teacher_norm = TEACHER_SCALE * jnp.sum(teacher_t * teacher_t, axis=0, keepdims=True)
            student_norm = STUDENT_SCALE * jnp.sum(student_t * student_t, axis=0, keepdims=True)
            norms += [teacher_norm, student_norm]
            high, low = split_high_low(teacher_t * TEACHER_SCALE)
            teacher_op = [high, low, teacher_gap, shift_rows(teacher_norm)]
            row_op[h, i, :, :rows] = jnp.concatenate(teacher_op, axis=0)
            high, low = split_high_low(student_t * STUDENT_SCALE)
            student_op = [student_gap, high, low, shift_rows(student_norm)]
            row_op[h, i, :, rows:] = jnp.concatenate(student_op, axis=0)

    safe = jnp.max(functools.reduce(jnp.maximum, norms)) <= SAFE_NORM
    key_pos = lax.broadcasted_iota(jnp.int32, (rows, rows), 0)
    row_pos = lax.broadcasted_iota(jnp.int32, (rows, rows), 1)

    def logits(h, i, j):
        keys = pl.ds(pl.multiple_of(j * rows, rows), rows)
        both = jnp.dot(key_op[h, keys, :], row_op[h, i], preferred_element_type=f32)
        return both[:, :rows], both[:, rows:]

    @pl.when(safe)
    def shifted_by_own_logit():
        key_grad[...] = jnp.zeros(key_grad.shape, f32)

        def exponentials(h, i, model, prob):
            upto = (i + 1) * rows
            depth = slice(2 * TEACHER_DIM if model else 0, DEPTH)
            op = row_op[h, i, depth, model * rows : (model + 1) * rows]
            values = jnp.dot(key_op[h, :upto, depth], op, preferred_element_type=f32)
            diagonal = jnp.where(key_pos <= row_pos, values[i * rows :], NEGATIVE)
            total = cross = jnp.zeros((8, rows), f32)
            for j in range(i + 1):
                value = diagonal if j == i else values[j * rows : (j + 1) * rows]
                exp = jnp.exp2(value)
                prob[i % 2, j] = exp
                total = total + fold(exp)
                weight = teacher_prob[i % 2, j] if model else exp
                cross = cross + fold(weight * value)
            return [jnp.sum(part, axis=0, keepdims=True) for part in (total, cross)]

        def weights(i, j, teacher_inv, student_inv):
            value = student_prob[i % 2, j] * student_inv - teacher_prob[i % 2, j] * teacher_inv
            weights_ref[j * rows : (j + 1) * rows, i * rows : (i + 1) * rows] = value.astype(bf16)

        def head_step(h, kl_total):
            inverse = None
            for i in range(tiles + 1):
                if i < tiles:
                    teacher_sum, teacher_cross = exponentials(h, i, 0, teacher_prob)
                    student_sum, student_cross = exponentials(h, i, 1, student_prob)
                if i:
                    upto = i * rows
                    for j in range(i):
                        weights(i - 1, j, *inverse)
                    row_grad[h, :, upto - rows : upto] = jnp.dot(
                        student_col[h, :, :upto],
                        weights_ref[:upto, upto - rows : upto],
                        preferred_element_type=f32,
                    )
                if i < tiles:
                    inverse = (1.0 / teacher_sum, 1.0 / student_sum)
                    kl_total = kl_total + (
                        (teacher_cross - student_cross) * inverse[0]
                        - jnp.log2(teacher_sum)
                        + jnp.log2(student_sum)
                    )
            for j in range(tiles):
                here = slice(j * rows, (j + 1) * rows)
                key_grad[here, :] = key_grad[here, :] + jnp.dot(
                    weights_ref[here, j * rows :],
                    student_pad[h, j * rows :, :],
                    preferred_element_type=f32,
                )
            return kl_total

        kl_sum[...] = lax.fori_loop(0, heads, head_step, jnp.zeros((1, rows), f32))

    @pl.when(jnp.logical_not(safe))
    def shifted_by_maximum():
        kl_sum[...] = jnp.zeros((1, rows), f32)
        key_grad[...] = jnp.zeros(key_grad.shape, f32)

        def masked(h, i, j):
            allowed = key_pos + j * rows <= row_pos + i * rows
            teacher, student = logits(h, i, j)
            return jnp.where(allowed, teacher, NEGATIVE), jnp.where(allowed, student, NEGATIVE)

        def row_step(step, _):
            h, i = step // tiles, step % tiles
            here = pl.ds(pl.multiple_of(i * rows, rows), rows)

            def advance(j, state):
                teacher_max, teacher_sum, cross_sum, student_max, student_sum = state
                teacher, student = masked(h, i, j)
                teacher_top = jnp.maximum(teacher_max, jnp.max(teacher, axis=0, keepdims=True))
                student_top = jnp.maximum(student_max, jnp.max(student, axis=0, keepdims=True))
                teacher_exp = jnp.exp2(teacher - teacher_top)
                student_exp = jnp.exp2(student - student_top)
                shrink = jnp.exp2(teacher_max - teacher_top)
                cross = jnp.sum(teacher_exp * (teacher - student), axis=0, keepdims=True)
                return (
                    teacher_top,
                    teacher_sum * shrink + jnp.sum(teacher_exp, axis=0, keepdims=True),
                    cross_sum * shrink + cross,
                    student_top,
                    student_sum * jnp.exp2(student_max - student_top)
                    + jnp.sum(student_exp, axis=0, keepdims=True),
                )

            lowest = jnp.full((1, rows), NEGATIVE, f32)
            zeros = jnp.zeros((1, rows), f32)
            teacher_max, teacher_sum, cross_sum, student_max, student_sum = lax.fori_loop(
                0, i + 1, advance, (lowest, zeros, zeros, lowest, zeros)
            )
            teacher_lse = teacher_max + jnp.log2(teacher_sum)
            student_lse = student_max + jnp.log2(student_sum)
            kl_sum[...] = kl_sum[...] + (cross_sum / teacher_sum - teacher_lse + student_lse)

            def spread(j, total):
                teacher, student = masked(h, i, j)
                value = jnp.exp2(student - student_lse) - jnp.exp2(teacher - teacher_lse)
                value = value.astype(bf16)
                keys = pl.ds(pl.multiple_of(j * rows, rows), rows)
                key_grad[keys, :] = key_grad[keys, :] + jnp.dot(
                    value, student_pad[h, here, :], preferred_element_type=f32
                )
                return total + jnp.dot(
                    student_col[h, :, keys], value, preferred_element_type=f32
                )

            row_grad[h, :, here] = lax.fori_loop(
                0, i + 1, spread, jnp.zeros((STUDENT_DIM, rows), f32)
            )
            return 0

        lax.fori_loop(0, heads * tiles, row_step, 0)

    if not last:
        return

    row_parts = [*done[::3], row_grad]
    key_parts = [*done[1::3], key_grad]
    total_width = len(row_parts) * student_width
    for i in range(tiles):
        here = slice(i * rows, (i + 1) * rows)
        columns = jnp.concatenate(
            [part[h, :, here] for part in row_parts for h in range(heads)], axis=0
        )
        lanes = jnp.concatenate([part[here, :] for part in key_parts], axis=1)
        grad_rows[here, :] = (columns.T + lanes) * (STUDENT_DIM**-0.5)
    grad_rows[pl.ds(live, window), :] = jnp.zeros((window, total_width), f32)
    kl_total = sum([ref[...] for ref in done[2::3]] + [kl_sum[...]])
    tokens = sum(counts_ref[b] for b in range(blocks))
    share = jnp.full((1, rows), math.log(2.0), f32) / (H_REL * tokens).astype(f32)
    kl_total = jnp.sum(kl_total * share, axis=1, keepdims=True)
    out[2][...] = jnp.broadcast_to(kl_total, out[2].shape)
    position = lax.broadcasted_iota(jnp.int32, (rows, window), 1)
    token = lax.broadcasted_iota(jnp.int32, (rows, window), 0)
    for k, (base, shift, count) in enumerate(places):
        place = ((position == token + shift) & (token < count)).astype(bf16)
        block = grad_rows[pl.ds(base, window), :].astype(bf16)
        out[k % 2][k // 2] = jnp.dot(place, block, preferred_element_type=f32).astype(bf16)


def local(teacher_queries, student_queries, token_counts):
    f32, bf16 = jnp.float32, jnp.bfloat16
    blocks = lax.axis_size("seq")
    chips = blocks // 2
    groups = lax.axis_size("head")
    rows = teacher_queries.shape[0]
    heads = teacher_queries.shape[1] // TEACHER_DIM // blocks
    tiles = blocks * 3 // 4
    live = tiles * rows
    folded = heads * STUDENT_DIM == LANES
    chunks = 2 if folded else 1
    chunk_heads = heads // chunks
    teacher_width = chunk_heads * TEACHER_DIM
    student_width = chunk_heads * STUDENT_DIM
    if folded:
        send_shape = (chips, rows + rows // 2, LANES)
    else:
        send_shape = (chips, rows, teacher_width + student_width)
    vmem = pl.BlockSpec(memory_space=pltpu.VMEM)
    smem = pl.BlockSpec(memory_space=pltpu.SMEM)
    params = pltpu.CompilerParams(vmem_limit_bytes=40 * 1024 * 1024)
    me = lax.axis_index("seq").reshape(1)
    far_first = sorted(range(1, chips), key=lambda k: -k.bit_count())

    def exchange(kept, swapped, kls=()):
        swapped = lax.ppermute(swapped, "seq", [(i, i ^ 1) for i in range(blocks)])
        shape = (2, kept.shape[1] + (TAIL if kls else 0), kept.shape[2])
        sends = pl.pallas_call(
            functools.partial(merge_kernel, chips),
            in_specs=[vmem] * (2 + len(kls)),
            out_specs=[vmem] * (chips - 1),
            out_shape=[jax.ShapeDtypeStruct(shape, bf16)] * (chips - 1),
            compiler_params=params,
            name="merge",
        )(kept, swapped, *kls)
        out = [None] * (chips - 1)
        for k in far_first:
            pairs = [(i, i ^ (2 * k)) for i in range(blocks)]
            out[k - 1] = lax.ppermute(sends[k - 1], "seq", pairs)
        return [kept, swapped] + out

    packed = jax.ShapeDtypeStruct(send_shape, bf16)
    first = jax.ShapeDtypeStruct(send_shape[1:], bf16)
    order = [0, 1, *range(2, blocks, 2), *range(3, blocks, 2)] if folded else None
    if folded:
        anywhere = pl.BlockSpec(memory_space=pltpu.HBM)
        sends = pl.pallas_call(
            functools.partial(pack_folded_kernel, blocks, chunks),
            in_specs=[smem, anywhere, anywhere],
            out_specs=[vmem] * (blocks + 2 * chunks - 2),
            out_shape=[first] * blocks + [packed] * (2 * chunks - 2),
            scratch_shapes=[
                pltpu.VMEM(student_queries.shape, bf16),
                pltpu.SemaphoreType.DMA((chunks * blocks + 1,)),
            ],
            compiler_params=pltpu.CompilerParams(vmem_limit_bytes=52 * 1024 * 1024),
            name="pack",
        )(me, teacher_queries, student_queries)
    else:
        sends = pl.pallas_call(
            functools.partial(pack_plain_kernel, blocks),
            in_specs=[smem, vmem, vmem],
            out_specs=[vmem] * 2,
            out_shape=[packed] * 2,
            compiler_params=params,
            name="pack",
        )(me, teacher_queries, student_queries)
    incoming = []
    if folded:
        incoming.append(
            [sends[0]]
            + [
                lax.ppermute(sends[k], "seq", [(i, i ^ k) for i in range(blocks)])
                for k in order[1:]
            ]
        )
        sends = sends[blocks:]
    incoming += [exchange(*pair) for pair in zip(sends[::2], sends[1::2])]

    result = [
        jax.ShapeDtypeStruct((chunk_heads, STUDENT_DIM, live), f32),
        jax.ShapeDtypeStruct((live, student_width), f32),
        jax.ShapeDtypeStruct((1, rows), f32),
    ]
    message = jax.ShapeDtypeStruct((chips, rows, heads * STUDENT_DIM), bf16)
    divergence = jax.ShapeDtypeStruct((1, heads * STUDENT_DIM), f32)
    pairs = chunk_heads * tiles * (tiles + 1) // 2 * rows * rows
    done = []
    for c in range(chunks):
        last = c == chunks - 1
        scratch = [
            pltpu.VMEM((live + rows + PAD, teacher_width + student_width), f32),
            pltpu.VMEM((chunk_heads, live, DEPTH), bf16),
            pltpu.VMEM((chunk_heads, tiles, DEPTH, 2 * rows), bf16),
            pltpu.VMEM((chunk_heads, STUDENT_DIM, live), bf16),
            pltpu.VMEM((chunk_heads, live, student_width), bf16),
            pltpu.VMEM((2, tiles, rows, rows), f32),
            pltpu.VMEM((2, tiles, rows, rows), f32),
            pltpu.VMEM((live, live), bf16),
        ]
        if last:
            scratch += [pltpu.VMEM(part.shape, f32) for part in result]
            scratch.append(pltpu.VMEM((live + rows + PAD, heads * STUDENT_DIM), f32))
        inputs = [me, token_counts, *incoming[c], *done]
        done += pl.pallas_call(
            functools.partial(
                relation_kernel,
                folded,
                chunk_heads,
                tiles,
                order if c == 0 else None,
                len(incoming[c]),
                c,
                last,
            ),
            in_specs=[smem, smem] + [vmem] * (len(inputs) - 2),
            out_specs=[vmem] * 3,
            out_shape=[message, message, divergence] if last else result,
            scratch_shapes=scratch,
            compiler_params=params,
            cost_estimate=pl.CostEstimate(
                flops=4 * pairs * DEPTH, bytes_accessed=8 * pairs, transcendentals=2 * pairs
            ),
            name="relation",
        )(*inputs)
    kept, swapped, kl = done[-3:]
    kl = kl + lax.ppermute(kl, "seq", [(i, i ^ 1) for i in range(blocks)])
    kls = [kl]
    for bit in range(groups.bit_length() - 1):
        own = pair_sum(kls)
        pairs = [(i, i ^ (1 << bit)) for i in range(groups)]
        kls = [own, lax.ppermute(own, "head", pairs)]
    returned = exchange(kept, swapped, kls)
    grad, loss = pl.pallas_call(
        functools.partial(unpack_kernel, len(kls)),
        in_specs=[smem] + [vmem] * (len(kls) + len(returned)),
        out_specs=[vmem] * 2,
        out_shape=[
            jax.ShapeDtypeStruct((rows, student_queries.shape[1]), f32),
            divergence,
        ],
        compiler_params=params,
        name="unpack",
    )(me, *kls, *returned)
    return (grad, loss[0, 0])


def solution(mesh):
    return jax.shard_map(
        local,
        mesh=mesh,
        in_specs=(P("seq", "head"), P("seq", "head"), P()),
        out_specs=(P("seq", "head"), P()),
        check_vma=False,
    )
```

profile of v0, /device:TPU:0, one launch (start us, length us, event | category | flops | bytes accessed | tf_op | source)
XLA Modules:
  0.0 80.1 jit_solution(15388196485919654836)
XLA Ops:
  0.6 1.5 %pack.1 = (bf16[384,128]{1,0:T(8,128)(2,1)S(1)}, bf16[384,128]{1,0:T(8,128)(2,1)S(1)}, bf16[384,128]{1,0:T(8,128)(2,1)S(1)}, bf16[384,128]{1,0:T(8,128)(2,1)S(1)...) custom-call(s32[1]{0:T(128)} %bitcast.me_ref, ...), custom_call_target="tpu_custom_call" | custom-call | tf_op jit(solution)/shard_map/pack/pallas_call | solution.py:437
  2.1 0.5 collective-permute-start
  2.6 0.1 collective-permute-start.4
  2.7 2.9 %collective-permute-start.5 = (bf16[384,128]{1,0:T(8,128)(2,1)S(1)}, bf16[384,128]{1,0:T(8,128)(2,1)S(1)}, u32[]{:S(2)}, u32[]{:S(2)}) collective-permute-start(bf16[384,128]{1,0:T(8,128)(2,1)S(1)} %get-tuple-element.33), channel_id=1, source_target_pairs={{0,8},{4,12},{8,0},{12,4},{16,24},{20,28},{24,16},{28,20},{1,9},{5... | collective-permute-start | bytes 294920 | tf_op jit(solution)/shard_map/ppermute | solution.py:463
  5.6 1.5 %collective-permute-start.6 = (bf16[384,128]{1,0:T(8,128)(2,1)S(1)}, bf16[384,128]{1,0:T(8,128)(2,1)S(1)}, u32[]{:S(2)}, u32[]{:S(2)}) collective-permute-start(bf16[384,128]{1,0:T(8,128)(2,1)S(1)} %get-tuple-element.34), channel_id=1, source_target_pairs={{0,16},{4,20},{8,24},{12,28},{16,0},{20,4},{24,8},{28,12},{1,17},{... | collective-permute-start | bytes 294920 | tf_op jit(solution)/shard_map/ppermute | solution.py:463
  7.2 0.0 collective-permute-start.7
  7.2 0.0 collective-permute-done.4.refs_1_
  7.2 0.8 %collective-permute-start.8 = (bf16[384,128]{1,0:T(8,128)(2,1)S(1)}, bf16[384,128]{1,0:T(8,128)(2,1)S(1)}, u32[]{:S(2)}, u32[]{:S(2)}) collective-permute-start(bf16[384,128]{1,0:T(8,128)(2,1)S(1)} %get-tuple-element.36), channel_id=1, source_target_pairs={{0,12},{4,8},{8,4},{12,0},{16,28},{20,24},{24,20},{28,16},{1,13},{... | collective-permute-start | bytes 294920 | tf_op jit(solution)/shard_map/ppermute | solution.py:463
  8.0 0.8 %collective-permute-done.5.refs_2_ = bf16[384,128]{1,0:T(8,128)(2,1)S(1)} collective-permute-done((bf16[384,128]{1,0:T(8,128)(2,1)S(1)}, bf16[384,128]{1,0:T(8,128)(2,1)S(1)}, u32[]{:S(2)}, u32[]{:S(2)}) %collective-permute-start.5) | collective-permute-done | bytes 98336 | tf_op jit(solution)/shard_map/ppermute | solution.py:463
  8.8 1.6 %collective-permute-start.9 = (bf16[384,128]{1,0:T(8,128)(2,1)S(1)}, bf16[384,128]{1,0:T(8,128)(2,1)S(1)}, u32[]{:S(2)}, u32[]{:S(2)}) collective-permute-start(bf16[384,128]{1,0:T(8,128)(2,1)S(1)} %get-tuple-element.37), channel_id=1, source_target_pairs={{0,20},{4,16},{8,28},{12,24},{16,4},{20,0},{24,12},{28,8},{1,21},{... | collective-permute-start | bytes 294920 | tf_op jit(solution)/shard_map/ppermute | solution.py:463
  10.4 0.0 collective-permute-done.swapped_ref.refs_1_
  10.4 2.1 %collective-permute-start.10 = (bf16[384,128]{1,0:T(8,128)(2,1)S(1)}, bf16[384,128]{1,0:T(8,128)(2,1)S(1)}, u32[]{:S(2)}, u32[]{:S(2)}) collective-permute-start(bf16[384,128]{1,0:T(8,128)(2,1)S(1)} %get-tuple-element.38), channel_id=1, source_target_pairs={{0,28},{4,24},{8,20},{12,16},{16,12},{20,8},{24,4},{28,0},{1,29},{... | collective-permute-start | bytes 294920 | tf_op jit(solution)/shard_map/ppermute | solution.py:463
  12.5 0.0 collective-permute-done.6.refs_3_
  12.5 0.1 collective-permute-start.1
  12.6 1.1 %collective-permute-done.7.refs_4_ = bf16[384,128]{1,0:T(8,128)(2,1)S(1)} collective-permute-done((bf16[384,128]{1,0:T(8,128)(2,1)S(1)}, bf16[384,128]{1,0:T(8,128)(2,1)S(1)}, u32[]{:S(2)}, u32[]{:S(2)}) %collective-permute-start.7) | collective-permute-done | bytes 98336 | tf_op jit(solution)/shard_map/ppermute | solution.py:463
  13.7 0.6 collective-permute-start.2
  14.3 0.0 collective-permute-done.8.refs_5_
  14.3 0.0 copy-start
  14.3 1.8 %collective-permute-start.3 = (bf16[2,384,128]{2,1,0:T(8,128)(2,1)S(1)}, bf16[2,384,128]{2,1,0:T(8,128)(2,1)S(1)}, u32[]{:S(2)}, u32[]{:S(2)}) collective-permute-start(bf16[2,384,128]{2,1,0:T(8,128)(2,1)S(1)} %get-tuple-element.30), channel_id=1, source_target_pairs={{0,24},{4,28},{8,16},{12,20},{16,8},{20,12},{24,0},{28,4},{1,25},{... | collective-permute-start | bytes 589832 | tf_op jit(solution)/shard_map/ppermute | solution.py:429
  16.1 0.0 collective-permute-done.9.refs_6_
  16.1 0.5 collective-permute-done.10.refs_7_
  16.5 0.0 copy-done
  16.5 9.6 %relation.2 = (f32[2,32,1536]{2,1,0:T(8,128)S(1)}, f32[1536,64]{1,0:T(8,128)S(1)}, f32[1,256]{1,0:T(1,128)S(1)}) custom-call(s32[1]{0:T(128)} %bitcast.me_ref, s32[8]{0:T(128)S(1)} %copy-done, bf16[384,128]{1,0:T(8,128)(2,1)S(1)} %get-tuple-element.31.refs_0_, bf16[384,128]{1,0:T(8,128)(2,1)S(1)} %collective-permute-done.4.refs_1_, ...), custom_call_target="tpu_custom_call" | custom-call | flops 2818572288 | bytes 22020096 | tf_op jit(solution)/shard_map/relation/pallas_call | solution.py:495
  26.2 0.0 collective-permute-done.1.refs_2_
  26.2 0.0 collective-permute-done.2.refs_3_
  26.2 0.0 collective-permute-done.3.refs_4_
  26.2 10.9 %relation.3 = (bf16[4,256,128]{2,1,0:T(8,128)(2,1)S(1)}, bf16[4,256,128]{2,1,0:T(8,128)(2,1)S(1)}, f32[1,128]{1,0:T(1,128)S(1)}) custom-call(s32[1]{0:T(128)} %bitcast.me_ref, s32[8]{0:T(128)S(1)} %copy-done, bf16[4,384,128]{2,1,0:T(8,128)(2,1)S(1)} %get-tuple-element.26.kept_ref.refs_0_, bf16[4,384,128]{2,1,0:T(8,128)(2,1)S(1)} %collective-permute-done.swapped_ref.refs_1_, ...), custom_call_target="tpu_custom_call" | custom-call | flops 2818572288 | bytes 22020096 | tf_op jit(solution)/shard_map/relation/pallas_call | solution.py:495
  37.2 0.7 collective-permute-start.14
  37.8 0.1 collective-permute-start.11
  37.9 1.1 %collective-permute-done.11 = f32[1,128]{1,0:T(1,128)S(1)} collective-permute-done((f32[1,128]{1,0:T(1,128)S(1)}, f32[1,128]{1,0:T(1,128)S(1)}, u32[]{:S(2)}, u32[]{:S(2)}) %collective-permute-start.11) | collective-permute-done | bytes 544 | tf_op jit(solution)/shard_map/ppermute | solution.py:517
  39.0 1.6 %collective-permute-start.12 = (f32[1,128]{1,0:T(1,128)S(1)}, f32[1,128]{1,0:T(1,128)S(1)}, u32[]{:S(2)}, u32[]{:S(2)}) collective-permute-start(f32[1,128]{1,0:T(1,128)S(1)} %add.6), channel_id=1, source_target_pairs={{0,1},{1,0},{2,3},{3,2},{4,5},{5,4},{6,7},{7,6},{8,9},{9,8},{10,11... | collective-permute-start | bytes 1544 | tf_op jit(solution)/shard_map/ppermute | solution.py:522
  40.6 2.0 %collective-permute-done.12 = f32[1,128]{1,0:T(1,128)S(1)} collective-permute-done((f32[1,128]{1,0:T(1,128)S(1)}, f32[1,128]{1,0:T(1,128)S(1)}, u32[]{:S(2)}, u32[]{:S(2)}) %collective-permute-start.12) | collective-permute-done | bytes 544 | tf_op jit(solution)/shard_map/ppermute | solution.py:522
  42.5 27.6 %collective-permute-start.13 = (f32[1,128]{1,0:T(1,128)S(1)}, f32[1,128]{1,0:T(1,128)S(1)}, u32[]{:S(2)}, u32[]{:S(2)}) collective-permute-start(f32[1,128]{1,0:T(1,128)S(1)} %add.7.refs_0_), channel_id=1, source_target_pairs={{0,2},{1,3},{2,0},{3,1},{4,6},{5,7},{6,4},{7,5},{8,10},{9,11},{10,... | collective-permute-start | bytes 1544 | tf_op jit(solution)/shard_map/ppermute | solution.py:522
  70.1 1.5 %collective-permute-done.13.refs_1_ = f32[1,128]{1,0:T(1,128)S(1)} collective-permute-done((f32[1,128]{1,0:T(1,128)S(1)}, f32[1,128]{1,0:T(1,128)S(1)}, u32[]{:S(2)}, u32[]{:S(2)}) %collective-permute-start.13) | collective-permute-done | bytes 544 | tf_op jit(solution)/shard_map/ppermute | solution.py:522
  71.6 0.0 collective-permute-done.14.swapped_ref.refs_3_
  71.7 0.1 collective-permute-start.15
  71.8 1.2 %collective-permute-start.16 = (bf16[2,272,128]{2,1,0:T(8,128)(2,1)S(1)}, bf16[2,272,128]{2,1,0:T(8,128)(2,1)S(1)}, u32[]{:S(2)}, u32[]{:S(2)}) collective-permute-start(bf16[2,272,128]{2,1,0:T(8,128)(2,1)S(1)} %get-tuple-element.46), channel_id=1, source_target_pairs={{0,16},{4,20},{8,24},{12,28},{16,0},{20,4},{24,8},{28,12},{1,17},{... | collective-permute-start | bytes 417800 | tf_op jit(solution)/shard_map/ppermute | solution.py:429
  72.9 2.3 %collective-permute-start.17 = (bf16[2,272,128]{2,1,0:T(8,128)(2,1)S(1)}, bf16[2,272,128]{2,1,0:T(8,128)(2,1)S(1)}, u32[]{:S(2)}, u32[]{:S(2)}) collective-permute-start(bf16[2,272,128]{2,1,0:T(8,128)(2,1)S(1)} %get-tuple-element.47), channel_id=1, source_target_pairs={{0,24},{4,28},{8,16},{12,20},{16,8},{20,12},{24,0},{28,4},{1,25},{... | collective-permute-start | bytes 417800 | tf_op jit(solution)/shard_map/ppermute | solution.py:429
  75.2 1.7 %collective-permute-done.15.refs_4_ = bf16[2,272,128]{2,1,0:T(8,128)(2,1)S(1)} collective-permute-done((bf16[2,272,128]{2,1,0:T(8,128)(2,1)S(1)}, bf16[2,272,128]{2,1,0:T(8,128)(2,1)S(1)}, u32[]{:S(2)}, u32[]{:S(2)}) %collective-permute-start.15) | collective-permute-done | bytes 139296 | tf_op jit(solution)/shard_map/ppermute | solution.py:429
  76.9 0.5 collective-permute-done.16.refs_5_
  77.5 1.5 %collective-permute-done.17.refs_6_ = bf16[2,272,128]{2,1,0:T(8,128)(2,1)S(1)} collective-permute-done((bf16[2,272,128]{2,1,0:T(8,128)(2,1)S(1)}, bf16[2,272,128]{2,1,0:T(8,128)(2,1)S(1)}, u32[]{:S(2)}, u32[]{:S(2)}) %collective-permute-start.17) | collective-permute-done | bytes 139296 | tf_op jit(solution)/shard_map/ppermute | solution.py:429
  79.0 1.1 %unpack.1 = (f32[256,1024]{1,0:T(8,128)}, f32[1,128]{1,0:T(1,128)}) custom-call(s32[1]{0:T(128)} %bitcast.me_ref, f32[1,128]{1,0:T(1,128)S(1)} %add.7.refs_0_, f32[1,128]{1,0:T(1,128)S(1)} %collective-permute-done.13.refs_1_, bf16[4,256,128]{2,1,0:T(8,128)(2,1)S(1)} %get-tuple-element.43.kept_ref.refs_2_, ...), custom_call_target="tpu_custom_call" | custom-call | tf_op jit(solution)/shard_map/unpack/pallas_call | solution.py:524
  (4 shorter events, 0.1 us)
Async XLA Ops:
  2.1 8.3 %collective-permute-start = (bf16[4,384,128]{2,1,0:T(8,128)(2,1)S(1)}, bf16[4,384,128]{2,1,0:T(8,128)(2,1)S(1)}, u32[]{:S(2)}, u32[]{:S(2)}) collective-permute-start(bf16[4,384,128]{2,1,0:T(8,128)(2,1)S(1)} %get-tuple-element.27), channel_id=1, source_target_pairs={{0,4},{4,0},{8,12},{12,8},{16,20},{20,16},{24,28},{28,24},{1,5},{5... | collective-permute-start | bytes 1179656 | tf_op jit(solution)/shard_map/ppermute | solution.py:416
  2.6 4.5 %collective-permute-start.4 = (bf16[384,128]{1,0:T(8,128)(2,1)S(1)}, bf16[384,128]{1,0:T(8,128)(2,1)S(1)}, u32[]{:S(2)}, u32[]{:S(2)}) collective-permute-start(bf16[384,128]{1,0:T(8,128)(2,1)S(1)} %get-tuple-element.32), channel_id=1, source_target_pairs={{0,4},{4,0},{8,12},{12,8},{16,20},{20,16},{24,28},{28,24},{1,5},{5... | collective-permute-start | bytes 294920 | tf_op jit(solution)/shard_map/ppermute | solution.py:463
  2.7 6.1 %collective-permute-start.5 = (bf16[384,128]{1,0:T(8,128)(2,1)S(1)}, bf16[384,128]{1,0:T(8,128)(2,1)S(1)}, u32[]{:S(2)}, u32[]{:S(2)}) collective-permute-start(bf16[384,128]{1,0:T(8,128)(2,1)S(1)} %get-tuple-element.33), channel_id=1, source_target_pairs={{0,8},{4,12},{8,0},{12,4},{16,24},{20,28},{24,16},{28,20},{1,9},{5... | collective-permute-start | bytes 294920 | tf_op jit(solution)/shard_map/ppermute | solution.py:463
  5.6 6.9 %collective-permute-start.6 = (bf16[384,128]{1,0:T(8,128)(2,1)S(1)}, bf16[384,128]{1,0:T(8,128)(2,1)S(1)}, u32[]{:S(2)}, u32[]{:S(2)}) collective-permute-start(bf16[384,128]{1,0:T(8,128)(2,1)S(1)} %get-tuple-element.34), channel_id=1, source_target_pairs={{0,16},{4,20},{8,24},{12,28},{16,0},{20,4},{24,8},{28,12},{1,17},{... | collective-permute-start | bytes 294920 | tf_op jit(solution)/shard_map/ppermute | solution.py:463
  7.2 6.5 %collective-permute-start.7 = (bf16[384,128]{1,0:T(8,128)(2,1)S(1)}, bf16[384,128]{1,0:T(8,128)(2,1)S(1)}, u32[]{:S(2)}, u32[]{:S(2)}) collective-permute-start(bf16[384,128]{1,0:T(8,128)(2,1)S(1)} %get-tuple-element.35), channel_id=1, source_target_pairs={{0,24},{4,28},{8,16},{12,20},{16,8},{20,12},{24,0},{28,4},{1,25},{... | collective-permute-start | bytes 294920 | tf_op jit(solution)/shard_map/ppermute | solution.py:463
  7.2 7.1 %collective-permute-start.8 = (bf16[384,128]{1,0:T(8,128)(2,1)S(1)}, bf16[384,128]{1,0:T(8,128)(2,1)S(1)}, u32[]{:S(2)}, u32[]{:S(2)}) collective-permute-start(bf16[384,128]{1,0:T(8,128)(2,1)S(1)} %get-tuple-element.36), channel_id=1, source_target_pairs={{0,12},{4,8},{8,4},{12,0},{16,28},{20,24},{24,20},{28,16},{1,13},{... | collective-permute-start | bytes 294920 | tf_op jit(solution)/shard_map/ppermute | solution.py:463
  8.8 7.3 %collective-permute-start.9 = (bf16[384,128]{1,0:T(8,128)(2,1)S(1)}, bf16[384,128]{1,0:T(8,128)(2,1)S(1)}, u32[]{:S(2)}, u32[]{:S(2)}) collective-permute-start(bf16[384,128]{1,0:T(8,128)(2,1)S(1)} %get-tuple-element.37), channel_id=1, source_target_pairs={{0,20},{4,16},{8,28},{12,24},{16,4},{20,0},{24,12},{28,8},{1,21},{... | collective-permute-start | bytes 294920 | tf_op jit(solution)/shard_map/ppermute | solution.py:463
  10.4 6.2 %collective-permute-start.10 = (bf16[384,128]{1,0:T(8,128)(2,1)S(1)}, bf16[384,128]{1,0:T(8,128)(2,1)S(1)}, u32[]{:S(2)}, u32[]{:S(2)}) collective-permute-start(bf16[384,128]{1,0:T(8,128)(2,1)S(1)} %get-tuple-element.38), channel_id=1, source_target_pairs={{0,28},{4,24},{8,20},{12,16},{16,12},{20,8},{24,4},{28,0},{1,29},{... | collective-permute-start | bytes 294920 | tf_op jit(solution)/shard_map/ppermute | solution.py:463
  12.5 13.7 %collective-permute-start.1 = (bf16[2,384,128]{2,1,0:T(8,128)(2,1)S(1)}, bf16[2,384,128]{2,1,0:T(8,128)(2,1)S(1)}, u32[]{:S(2)}, u32[]{:S(2)}) collective-permute-start(bf16[2,384,128]{2,1,0:T(8,128)(2,1)S(1)} %get-tuple-element.28), channel_id=1, source_target_pairs={{0,8},{4,12},{8,0},{12,4},{16,24},{20,28},{24,16},{28,20},{1,9},{5... | collective-permute-start | bytes 589832 | tf_op jit(solution)/shard_map/ppermute | solution.py:429
  13.7 12.5 %collective-permute-start.2 = (bf16[2,384,128]{2,1,0:T(8,128)(2,1)S(1)}, bf16[2,384,128]{2,1,0:T(8,128)(2,1)S(1)}, u32[]{:S(2)}, u32[]{:S(2)}) collective-permute-start(bf16[2,384,128]{2,1,0:T(8,128)(2,1)S(1)} %get-tuple-element.29), channel_id=1, source_target_pairs={{0,16},{4,20},{8,24},{12,28},{16,0},{20,4},{24,8},{28,12},{1,17},{... | collective-permute-start | bytes 589832 | tf_op jit(solution)/shard_map/ppermute | solution.py:429
  14.3 2.3 %copy-start = (s32[8]{0:T(128)S(1)}, s32[8]{0:T(128)}, u32[]{:S(2)}) copy-start(s32[8]{0:T(128)} %counts_ref.3) | copy-start | bytes 100
  14.3 11.9 %collective-permute-start.3 = (bf16[2,384,128]{2,1,0:T(8,128)(2,1)S(1)}, bf16[2,384,128]{2,1,0:T(8,128)(2,1)S(1)}, u32[]{:S(2)}, u32[]{:S(2)}) collective-permute-start(bf16[2,384,128]{2,1,0:T(8,128)(2,1)S(1)} %get-tuple-element.30), channel_id=1, source_target_pairs={{0,24},{4,28},{8,16},{12,20},{16,8},{20,12},{24,0},{28,4},{1,25},{... | collective-permute-start | bytes 589832 | tf_op jit(solution)/shard_map/ppermute | solution.py:429
  37.2 34.5 %collective-permute-start.14 = (bf16[4,256,128]{2,1,0:T(8,128)(2,1)S(1)}, bf16[4,256,128]{2,1,0:T(8,128)(2,1)S(1)}, u32[]{:S(2)}, u32[]{:S(2)}) collective-permute-start(bf16[4,256,128]{2,1,0:T(8,128)(2,1)S(1)} %get-tuple-element.44), channel_id=1, source_target_pairs={{0,4},{4,0},{8,12},{12,8},{16,20},{20,16},{24,28},{28,24},{1,5},{5... | collective-permute-start | bytes 786440 | tf_op jit(solution)/shard_map/ppermute | solution.py:416
  37.8 1.2 %collective-permute-start.11 = (f32[1,128]{1,0:T(1,128)S(1)}, f32[1,128]{1,0:T(1,128)S(1)}, u32[]{:S(2)}, u32[]{:S(2)}) collective-permute-start(f32[1,128]{1,0:T(1,128)S(1)} %get-tuple-element.42), channel_id=1, source_target_pairs={{0,4},{4,0},{8,12},{12,8},{16,20},{20,16},{24,28},{28,24},{1,5},{5... | collective-permute-start | bytes 1544 | tf_op jit(solution)/shard_map/ppermute | solution.py:517
  39.0 3.6 %collective-permute-start.12 = (f32[1,128]{1,0:T(1,128)S(1)}, f32[1,128]{1,0:T(1,128)S(1)}, u32[]{:S(2)}, u32[]{:S(2)}) collective-permute-start(f32[1,128]{1,0:T(1,128)S(1)} %add.6), channel_id=1, source_target_pairs={{0,1},{1,0},{2,3},{3,2},{4,5},{5,4},{6,7},{7,6},{8,9},{9,8},{10,11... | collective-permute-start | bytes 1544 | tf_op jit(solution)/shard_map/ppermute | solution.py:522
  42.5 29.1 %collective-permute-start.13 = (f32[1,128]{1,0:T(1,128)S(1)}, f32[1,128]{1,0:T(1,128)S(1)}, u32[]{:S(2)}, u32[]{:S(2)}) collective-permute-start(f32[1,128]{1,0:T(1,128)S(1)} %add.7.refs_0_), channel_id=1, source_target_pairs={{0,2},{1,3},{2,0},{3,1},{4,6},{5,7},{6,4},{7,5},{8,10},{9,11},{10,... | collective-permute-start | bytes 1544 | tf_op jit(solution)/shard_map/ppermute | solution.py:522
  71.7 5.3 %collective-permute-start.15 = (bf16[2,272,128]{2,1,0:T(8,128)(2,1)S(1)}, bf16[2,272,128]{2,1,0:T(8,128)(2,1)S(1)}, u32[]{:S(2)}, u32[]{:S(2)}) collective-permute-start(bf16[2,272,128]{2,1,0:T(8,128)(2,1)S(1)} %get-tuple-element.45), channel_id=1, source_target_pairs={{0,8},{4,12},{8,0},{12,4},{16,24},{20,28},{24,16},{28,20},{1,9},{5... | collective-permute-start | bytes 417800 | tf_op jit(solution)/shard_map/ppermute | solution.py:429
  71.8 5.7 %collective-permute-start.16 = (bf16[2,272,128]{2,1,0:T(8,128)(2,1)S(1)}, bf16[2,272,128]{2,1,0:T(8,128)(2,1)S(1)}, u32[]{:S(2)}, u32[]{:S(2)}) collective-permute-start(bf16[2,272,128]{2,1,0:T(8,128)(2,1)S(1)} %get-tuple-element.46), channel_id=1, source_target_pairs={{0,16},{4,20},{8,24},{12,28},{16,0},{20,4},{24,8},{28,12},{1,17},{... | collective-permute-start | bytes 417800 | tf_op jit(solution)/shard_map/ppermute | solution.py:429
  72.9 6.0 %collective-permute-start.17 = (bf16[2,272,128]{2,1,0:T(8,128)(2,1)S(1)}, bf16[2,272,128]{2,1,0:T(8,128)(2,1)S(1)}, u32[]{:S(2)}, u32[]{:S(2)}) collective-permute-start(bf16[2,272,128]{2,1,0:T(8,128)(2,1)S(1)} %get-tuple-element.47), channel_id=1, source_target_pairs={{0,24},{4,28},{8,16},{12,20},{16,8},{20,12},{24,0},{28,4},{1,25},{... | collective-permute-start | bytes 417800 | tf_op jit(solution)/shard_map/ppermute | solution.py:429
where the time goes:
time: 80.5 us; the launch traced here: 80.1 us
  starting transfers between devices  45.4 us (56%)
  Pallas kernels  23.2 us (29%)
  waiting for transfers between devices  10.7 us (13%)
    ppermute x2, starting transfers between devices, local(): kls = [own, lax.ppermute(own, 'head', pairs)]  29.2 us
    pallas_call x2, Pallas kernels, local(): pl.pallas_call(functools.partial(relation_kernel, folded, chunk_heads, ti...  20.6 us
    ppermute x7, starting transfers between devices, local(): lax.ppermute(sends[k], 'seq', [(i, i ^ k) for i in range(blocks)])  8.99 us
    ppermute x6, starting transfers between devices, exchange(): out[k - 1] = lax.ppermute(sends[k - 1], 'seq', pairs)  6 us
    ppermute x6, waiting for transfers between devices, exchange(): out[k - 1] = lax.ppermute(sends[k - 1], 'seq', pairs)  3.74 us
    ppermute x2, waiting for transfers between devices, local(): kls = [own, lax.ppermute(own, 'head', pairs)]  3.49 us
    ppermute x7, waiting for transfers between devices, local(): lax.ppermute(sends[k], 'seq', [(i, i ^ k) for i in range(blocks)])  2.38 us
  transfers between devices with their start and end apart: 18, of which 9 were waited for; matrix products, arithmetic and copies ran while one was open for 0% of the time, Pallas kernels for 12%

commit v1 on v0

--- a/solution.py
+++ b/solution.py
@@ -253,15 +253,27 @@
             depth = slice(2 * TEACHER_DIM if model else 0, DEPTH)
             op = row_op[h, i, depth, model * rows : (model + 1) * rows]
             values = jnp.dot(key_op[h, :upto, depth], op, preferred_element_type=f32)
-            diagonal = jnp.where(key_pos <= row_pos, values[i * rows :], NEGATIVE)
             total = cross = jnp.zeros((8, rows), f32)
-            for j in range(i + 1):
-                value = diagonal if j == i else values[j * rows : (j + 1) * rows]
+            for j in range(i):
+                value = values[j * rows : (j + 1) * rows]
                 exp = jnp.exp2(value)
                 prob[i % 2, j] = exp
                 total = total + fold(exp)
                 weight = teacher_prob[i % 2, j] if model else exp
                 cross = cross + fold(weight * value)
+            diagonal = jnp.where(key_pos <= row_pos, values[i * rows :], NEGATIVE)
+            half = rows // 2
+            prob[i % 2, i, half:, :half] = jnp.zeros((half, half), f32)
+            gap = jnp.zeros((8, half), f32)
+            for keys, here in ((slice(0, half), slice(0, rows)), (slice(half, rows),) * 2):
+                value = diagonal[keys, here]
+                exp = jnp.exp2(value)
+                prob[i % 2, i, keys, here] = exp
+                weight = teacher_prob[i % 2, i, keys, here] if model else exp
+                sums = [fold(exp), fold(weight * value)]
+                if keys.start:
+                    sums = [jnp.concatenate([gap, part], axis=1) for part in sums]
+                total, cross = total + sums[0], cross + sums[1]
             return [jnp.sum(part, axis=0, keepdims=True) for part in (total, cross)]
 
         def weights(i, j, teacher_inv, student_inv):

time: 80.5 us -> 80.4 us (level)
  transfers between devices with their start and end apart: 18 -> 18, of which waited for: 9 -> 8; matrix products, arithmetic and copies ran while one was open for 0% -> 0% of each run, Pallas kernels for 12% -> 12%
where the time goes in v1:
time: 80.4 us; the launch traced here: 79.4 us
  starting transfers between devices  45 us (56%)
  Pallas kernels  23.2 us (29%)
  waiting for transfers between devices  10.5 us (13%)
    ppermute x2, starting transfers between devices, local(): kls = [own, lax.ppermute(own, 'head', pairs)]  28.8 us
    pallas_call x2, Pallas kernels, local(): pl.pallas_call(functools.partial(relation_kernel, folded, chunk_heads, ti...  20.5 us
    ppermute x7, starting transfers between devices, local(): lax.ppermute(sends[k], 'seq', [(i, i ^ k) for i in range(blocks)])  8.99 us
    ppermute x6, starting transfers between devices, exchange(): out[k - 1] = lax.ppermute(sends[k - 1], 'seq', pairs)  5.99 us
    ppermute x6, waiting for transfers between devices, exchange(): out[k - 1] = lax.ppermute(sends[k - 1], 'seq', pairs)  3.56 us
    ppermute x2, waiting for transfers between devices, local(): kls = [own, lax.ppermute(own, 'head', pairs)]  3.49 us
    ppermute x7, waiting for transfers between devices, local(): lax.ppermute(sends[k], 'seq', [(i, i ^ k) for i in range(blocks)])  2.38 us
  transfers between devices with their start and end apart: 18, of which 8 were waited for; matrix products, arithmetic and copies ran while one was open for 0% of the time, Pallas kernels for 12%

profile of v1, /device:TPU:0, one launch (start us, length us, event | category | flops | bytes accessed | tf_op | source)
XLA Modules:
  0.0 79.4 jit_solution(13809401693003426524)
XLA Ops:
  0.6 1.5 %pack.1 = (bf16[384,128]{1,0:T(8,128)(2,1)S(1)}, bf16[384,128]{1,0:T(8,128)(2,1)S(1)}, bf16[384,128]{1,0:T(8,128)(2,1)S(1)}, bf16[384,128]{1,0:T(8,128)(2,1)S(1)...) custom-call(s32[1]{0:T(128)} %bitcast.me_ref, ...), custom_call_target="tpu_custom_call" | custom-call | tf_op jit(solution)/shard_map/pack/pallas_call | solution.py:449
  2.1 0.5 collective-permute-start
  2.6 0.1 collective-permute-start.4
  2.7 2.9 %collective-permute-start.5 = (bf16[384,128]{1,0:T(8,128)(2,1)S(1)}, bf16[384,128]{1,0:T(8,128)(2,1)S(1)}, u32[]{:S(2)}, u32[]{:S(2)}) collective-permute-start(bf16[384,128]{1,0:T(8,128)(2,1)S(1)} %get-tuple-element.33), channel_id=1, source_target_pairs={{0,8},{4,12},{8,0},{12,4},{16,24},{20,28},{24,16},{28,20},{1,9},{5... | collective-permute-start | bytes 294920 | tf_op jit(solution)/shard_map/ppermute | solution.py:475
  5.6 1.5 %collective-permute-start.6 = (bf16[384,128]{1,0:T(8,128)(2,1)S(1)}, bf16[384,128]{1,0:T(8,128)(2,1)S(1)}, u32[]{:S(2)}, u32[]{:S(2)}) collective-permute-start(bf16[384,128]{1,0:T(8,128)(2,1)S(1)} %get-tuple-element.34), channel_id=1, source_target_pairs={{0,16},{4,20},{8,24},{12,28},{16,0},{20,4},{24,8},{28,12},{1,17},{... | collective-permute-start | bytes 294920 | tf_op jit(solution)/shard_map/ppermute | solution.py:475
  7.2 0.0 collective-permute-start.7
  7.2 0.0 collective-permute-done.4.refs_1_
  7.2 0.8 %collective-permute-start.8 = (bf16[384,128]{1,0:T(8,128)(2,1)S(1)}, bf16[384,128]{1,0:T(8,128)(2,1)S(1)}, u32[]{:S(2)}, u32[]{:S(2)}) collective-permute-start(bf16[384,128]{1,0:T(8,128)(2,1)S(1)} %get-tuple-element.36), channel_id=1, source_target_pairs={{0,12},{4,8},{8,4},{12,0},{16,28},{20,24},{24,20},{28,16},{1,13},{... | collective-permute-start | bytes 294920 | tf_op jit(solution)/shard_map/ppermute | solution.py:475
  8.0 0.8 %collective-permute-done.5.refs_2_ = bf16[384,128]{1,0:T(8,128)(2,1)S(1)} collective-permute-done((bf16[384,128]{1,0:T(8,128)(2,1)S(1)}, bf16[384,128]{1,0:T(8,128)(2,1)S(1)}, u32[]{:S(2)}, u32[]{:S(2)}) %collective-permute-start.5) | collective-permute-done | bytes 98336 | tf_op jit(solution)/shard_map/ppermute | solution.py:475
  8.8 1.6 %collective-permute-start.9 = (bf16[384,128]{1,0:T(8,128)(2,1)S(1)}, bf16[384,128]{1,0:T(8,128)(2,1)S(1)}, u32[]{:S(2)}, u32[]{:S(2)}) collective-permute-start(bf16[384,128]{1,0:T(8,128)(2,1)S(1)} %get-tuple-element.37), channel_id=1, source_target_pairs={{0,20},{4,16},{8,28},{12,24},{16,4},{20,0},{24,12},{28,8},{1,21},{... | collective-permute-start | bytes 294920 | tf_op jit(solution)/shard_map/ppermute | solution.py:475
  10.4 0.0 collective-permute-done.swapped_ref.refs_1_
  10.4 2.1 %collective-permute-start.10 = (bf16[384,128]{1,0:T(8,128)(2,1)S(1)}, bf16[384,128]{1,0:T(8,128)(2,1)S(1)}, u32[]{:S(2)}, u32[]{:S(2)}) collective-permute-start(bf16[384,128]{1,0:T(8,128)(2,1)S(1)} %get-tuple-element.38), channel_id=1, source_target_pairs={{0,28},{4,24},{8,20},{12,16},{16,12},{20,8},{24,4},{28,0},{1,29},{... | collective-permute-start | bytes 294920 | tf_op jit(solution)/shard_map/ppermute | solution.py:475
  12.5 0.0 collective-permute-done.6.refs_3_
  12.5 0.1 collective-permute-start.1
  12.6 1.1 %collective-permute-done.7.refs_4_ = bf16[384,128]{1,0:T(8,128)(2,1)S(1)} collective-permute-done((bf16[384,128]{1,0:T(8,128)(2,1)S(1)}, bf16[384,128]{1,0:T(8,128)(2,1)S(1)}, u32[]{:S(2)}, u32[]{:S(2)}) %collective-permute-start.7) | collective-permute-done | bytes 98336 | tf_op jit(solution)/shard_map/ppermute | solution.py:475
  13.7 0.6 collective-permute-start.2
  14.3 0.0 collective-permute-done.8.refs_5_
  14.3 0.0 copy-start
  14.3 1.8 %collective-permute-start.3 = (bf16[2,384,128]{2,1,0:T(8,128)(2,1)S(1)}, bf16[2,384,128]{2,1,0:T(8,128)(2,1)S(1)}, u32[]{:S(2)}, u32[]{:S(2)}) collective-permute-start(bf16[2,384,128]{2,1,0:T(8,128)(2,1)S(1)} %get-tuple-element.30), channel_id=1, source_target_pairs={{0,24},{4,28},{8,16},{12,20},{16,8},{20,12},{24,0},{28,4},{1,25},{... | collective-permute-start | bytes 589832 | tf_op jit(solution)/shard_map/ppermute | solution.py:441
  16.1 0.0 collective-permute-done.9.refs_6_
  16.1 0.5 collective-permute-done.10.refs_7_
  16.5 0.0 copy-done
  16.5 9.6 %relation.2 = (f32[2,32,1536]{2,1,0:T(8,128)S(1)}, f32[1536,64]{1,0:T(8,128)S(1)}, f32[1,256]{1,0:T(1,128)S(1)}) custom-call(s32[1]{0:T(128)} %bitcast.me_ref, s32[8]{0:T(128)S(1)} %copy-done, bf16[384,128]{1,0:T(8,128)(2,1)S(1)} %get-tuple-element.31.refs_0_, bf16[384,128]{1,0:T(8,128)(2,1)S(1)} %collective-permute-done.4.refs_1_, ...), custom_call_target="tpu_custom_call" | custom-call | flops 2818572288 | bytes 22020096 | tf_op jit(solution)/shard_map/relation/pallas_call | solution.py:507
  26.1 0.0 collective-permute-done.1.refs_2_
  26.2 0.0 collective-permute-done.2.refs_3_
  26.2 0.0 collective-permute-done.3.refs_4_
  26.2 10.9 %relation.3 = (bf16[4,256,128]{2,1,0:T(8,128)(2,1)S(1)}, bf16[4,256,128]{2,1,0:T(8,128)(2,1)S(1)}, f32[1,128]{1,0:T(1,128)S(1)}) custom-call(s32[1]{0:T(128)} %bitcast.me_ref, s32[8]{0:T(128)S(1)} %copy-done, bf16[4,384,128]{2,1,0:T(8,128)(2,1)S(1)} %get-tuple-element.26.kept_ref.refs_0_, bf16[4,384,128]{2,1,0:T(8,128)(2,1)S(1)} %collective-permute-done.swapped_ref.refs_1_, ...), custom_call_target="tpu_custom_call" | custom-call | flops 2818572288 | bytes 22020096 | tf_op jit(solution)/shard_map/relation/pallas_call | solution.py:507
  37.1 0.6 collective-permute-start.14
  37.7 0.1 collective-permute-start.11
  37.8 1.1 %collective-permute-done.11 = f32[1,128]{1,0:T(1,128)S(1)} collective-permute-done((f32[1,128]{1,0:T(1,128)S(1)}, f32[1,128]{1,0:T(1,128)S(1)}, u32[]{:S(2)}, u32[]{:S(2)}) %collective-permute-start.11) | collective-permute-done | bytes 544 | tf_op jit(solution)/shard_map/ppermute | solution.py:529
  38.9 1.6 %collective-permute-start.12 = (f32[1,128]{1,0:T(1,128)S(1)}, f32[1,128]{1,0:T(1,128)S(1)}, u32[]{:S(2)}, u32[]{:S(2)}) collective-permute-start(f32[1,128]{1,0:T(1,128)S(1)} %add.6), channel_id=1, source_target_pairs={{0,1},{1,0},{2,3},{3,2},{4,5},{5,4},{6,7},{7,6},{8,9},{9,8},{10,11... | collective-permute-start | bytes 1544 | tf_op jit(solution)/shard_map/ppermute | solution.py:534
  40.5 2.0 %collective-permute-done.12 = f32[1,128]{1,0:T(1,128)S(1)} collective-permute-done((f32[1,128]{1,0:T(1,128)S(1)}, f32[1,128]{1,0:T(1,128)S(1)}, u32[]{:S(2)}, u32[]{:S(2)}) %collective-permute-start.12) | collective-permute-done | bytes 544 | tf_op jit(solution)/shard_map/ppermute | solution.py:534
  42.5 27.2 %collective-permute-start.13 = (f32[1,128]{1,0:T(1,128)S(1)}, f32[1,128]{1,0:T(1,128)S(1)}, u32[]{:S(2)}, u32[]{:S(2)}) collective-permute-start(f32[1,128]{1,0:T(1,128)S(1)} %add.7.refs_0_), channel_id=1, source_target_pairs={{0,2},{1,3},{2,0},{3,1},{4,6},{5,7},{6,4},{7,5},{8,10},{9,11},{10,... | collective-permute-start | bytes 1544 | tf_op jit(solution)/shard_map/ppermute | solution.py:534
  69.7 1.5 %collective-permute-done.13.refs_1_ = f32[1,128]{1,0:T(1,128)S(1)} collective-permute-done((f32[1,128]{1,0:T(1,128)S(1)}, f32[1,128]{1,0:T(1,128)S(1)}, u32[]{:S(2)}, u32[]{:S(2)}) %collective-permute-start.13) | collective-permute-done | bytes 544 | tf_op jit(solution)/shard_map/ppermute | solution.py:534
  71.2 0.0 collective-permute-done.14.swapped_ref.refs_3_
  71.2 0.1 collective-permute-start.15
  71.3 0.1 collective-permute-start.16
  71.4 3.4 %collective-permute-start.17 = (bf16[2,272,128]{2,1,0:T(8,128)(2,1)S(1)}, bf16[2,272,128]{2,1,0:T(8,128)(2,1)S(1)}, u32[]{:S(2)}, u32[]{:S(2)}) collective-permute-start(bf16[2,272,128]{2,1,0:T(8,128)(2,1)S(1)} %get-tuple-element.47), channel_id=1, source_target_pairs={{0,24},{4,28},{8,16},{12,20},{16,8},{20,12},{24,0},{28,4},{1,25},{... | collective-permute-start | bytes 417800 | tf_op jit(solution)/shard_map/ppermute | solution.py:441
  74.8 2.0 %collective-permute-done.15.refs_4_ = bf16[2,272,128]{2,1,0:T(8,128)(2,1)S(1)} collective-permute-done((bf16[2,272,128]{2,1,0:T(8,128)(2,1)S(1)}, bf16[2,272,128]{2,1,0:T(8,128)(2,1)S(1)}, u32[]{:S(2)}, u32[]{:S(2)}) %collective-permute-start.15) | collective-permute-done | bytes 139296 | tf_op jit(solution)/shard_map/ppermute | solution.py:441
  76.8 1.5 %collective-permute-done.16.refs_5_ = bf16[2,272,128]{2,1,0:T(8,128)(2,1)S(1)} collective-permute-done((bf16[2,272,128]{2,1,0:T(8,128)(2,1)S(1)}, bf16[2,272,128]{2,1,0:T(8,128)(2,1)S(1)}, u32[]{:S(2)}, u32[]{:S(2)}) %collective-permute-start.16) | collective-permute-done | bytes 139296 | tf_op jit(solution)/shard_map/ppermute | solution.py:441
  78.3 0.0 collective-permute-done.17.refs_6_
  78.3 1.1 %unpack.1 = (f32[256,1024]{1,0:T(8,128)}, f32[1,128]{1,0:T(1,128)}) custom-call(s32[1]{0:T(128)} %bitcast.me_ref, f32[1,128]{1,0:T(1,128)S(1)} %add.7.refs_0_, f32[1,128]{1,0:T(1,128)S(1)} %collective-permute-done.13.refs_1_, bf16[4,256,128]{2,1,0:T(8,128)(2,1)S(1)} %get-tuple-element.43.kept_ref.refs_2_, ...), custom_call_target="tpu_custom_call" | custom-call | tf_op jit(solution)/shard_map/unpack/pallas_call | solution.py:536
  (4 shorter events, 0.1 us)
Async XLA Ops:
  2.1 8.3 %collective-permute-start = (bf16[4,384,128]{2,1,0:T(8,128)(2,1)S(1)}, bf16[4,384,128]{2,1,0:T(8,128)(2,1)S(1)}, u32[]{:S(2)}, u32[]{:S(2)}) collective-permute-start(bf16[4,384,128]{2,1,0:T(8,128)(2,1)S(1)} %get-tuple-element.27), channel_id=1, source_target_pairs={{0,4},{4,0},{8,12},{12,8},{16,20},{20,16},{24,28},{28,24},{1,5},{5... | collective-permute-start | bytes 1179656 | tf_op jit(solution)/shard_map/ppermute | solution.py:428
  2.6 4.5 %collective-permute-start.4 = (bf16[384,128]{1,0:T(8,128)(2,1)S(1)}, bf16[384,128]{1,0:T(8,128)(2,1)S(1)}, u32[]{:S(2)}, u32[]{:S(2)}) collective-permute-start(bf16[384,128]{1,0:T(8,128)(2,1)S(1)} %get-tuple-element.32), channel_id=1, source_target_pairs={{0,4},{4,0},{8,12},{12,8},{16,20},{20,16},{24,28},{28,24},{1,5},{5... | collective-permute-start | bytes 294920 | tf_op jit(solution)/shard_map/ppermute | solution.py:475
  2.7 6.1 %collective-permute-start.5 = (bf16[384,128]{1,0:T(8,128)(2,1)S(1)}, bf16[384,128]{1,0:T(8,128)(2,1)S(1)}, u32[]{:S(2)}, u32[]{:S(2)}) collective-permute-start(bf16[384,128]{1,0:T(8,128)(2,1)S(1)} %get-tuple-element.33), channel_id=1, source_target_pairs={{0,8},{4,12},{8,0},{12,4},{16,24},{20,28},{24,16},{28,20},{1,9},{5... | collective-permute-start | bytes 294920 | tf_op jit(solution)/shard_map/ppermute | solution.py:475
  5.6 6.9 %collective-permute-start.6 = (bf16[384,128]{1,0:T(8,128)(2,1)S(1)}, bf16[384,128]{1,0:T(8,128)(2,1)S(1)}, u32[]{:S(2)}, u32[]{:S(2)}) collective-permute-start(bf16[384,128]{1,0:T(8,128)(2,1)S(1)} %get-tuple-element.34), channel_id=1, source_target_pairs={{0,16},{4,20},{8,24},{12,28},{16,0},{20,4},{24,8},{28,12},{1,17},{... | collective-permute-start | bytes 294920 | tf_op jit(solution)/shard_map/ppermute | solution.py:475
  7.2 6.5 %collective-permute-start.7 = (bf16[384,128]{1,0:T(8,128)(2,1)S(1)}, bf16[384,128]{1,0:T(8,128)(2,1)S(1)}, u32[]{:S(2)}, u32[]{:S(2)}) collective-permute-start(bf16[384,128]{1,0:T(8,128)(2,1)S(1)} %get-tuple-element.35), channel_id=1, source_target_pairs={{0,24},{4,28},{8,16},{12,20},{16,8},{20,12},{24,0},{28,4},{1,25},{... | collective-permute-start | bytes 294920 | tf_op jit(solution)/shard_map/ppermute | solution.py:475
  7.2 7.1 %collective-permute-start.8 = (bf16[384,128]{1,0:T(8,128)(2,1)S(1)}, bf16[384,128]{1,0:T(8,128)(2,1)S(1)}, u32[]{:S(2)}, u32[]{:S(2)}) collective-permute-start(bf16[384,128]{1,0:T(8,128)(2,1)S(1)} %get-tuple-element.36), channel_id=1, source_target_pairs={{0,12},{4,8},{8,4},{12,0},{16,28},{20,24},{24,20},{28,16},{1,13},{... | collective-permute-start | bytes 294920 | tf_op jit(solution)/shard_map/ppermute | solution.py:475
  8.8 7.3 %collective-permute-start.9 = (bf16[384,128]{1,0:T(8,128)(2,1)S(1)}, bf16[384,128]{1,0:T(8,128)(2,1)S(1)}, u32[]{:S(2)}, u32[]{:S(2)}) collective-permute-start(bf16[384,128]{1,0:T(8,128)(2,1)S(1)} %get-tuple-element.37), channel_id=1, source_target_pairs={{0,20},{4,16},{8,28},{12,24},{16,4},{20,0},{24,12},{28,8},{1,21},{... | collective-permute-start | bytes 294920 | tf_op jit(solution)/shard_map/ppermute | solution.py:475
  10.4 6.2 %collective-permute-start.10 = (bf16[384,128]{1,0:T(8,128)(2,1)S(1)}, bf16[384,128]{1,0:T(8,128)(2,1)S(1)}, u32[]{:S(2)}, u32[]{:S(2)}) collective-permute-start(bf16[384,128]{1,0:T(8,128)(2,1)S(1)} %get-tuple-element.38), channel_id=1, source_target_pairs={{0,28},{4,24},{8,20},{12,16},{16,12},{20,8},{24,4},{28,0},{1,29},{... | collective-permute-start | bytes 294920 | tf_op jit(solution)/shard_map/ppermute | solution.py:475
  12.5 13.6 %collective-permute-start.1 = (bf16[2,384,128]{2,1,0:T(8,128)(2,1)S(1)}, bf16[2,384,128]{2,1,0:T(8,128)(2,1)S(1)}, u32[]{:S(2)}, u32[]{:S(2)}) collective-permute-start(bf16[2,384,128]{2,1,0:T(8,128)(2,1)S(1)} %get-tuple-element.28), channel_id=1, source_target_pairs={{0,8},{4,12},{8,0},{12,4},{16,24},{20,28},{24,16},{28,20},{1,9},{5... | collective-permute-start | bytes 589832 | tf_op jit(solution)/shard_map/ppermute | solution.py:441
  13.7 12.5 %collective-permute-start.2 = (bf16[2,384,128]{2,1,0:T(8,128)(2,1)S(1)}, bf16[2,384,128]{2,1,0:T(8,128)(2,1)S(1)}, u32[]{:S(2)}, u32[]{:S(2)}) collective-permute-start(bf16[2,384,128]{2,1,0:T(8,128)(2,1)S(1)} %get-tuple-element.29), channel_id=1, source_target_pairs={{0,16},{4,20},{8,24},{12,28},{16,0},{20,4},{24,8},{28,12},{1,17},{... | collective-permute-start | bytes 589832 | tf_op jit(solution)/shard_map/ppermute | solution.py:441
  14.3 2.3 %copy-start = (s32[8]{0:T(128)S(1)}, s32[8]{0:T(128)}, u32[]{:S(2)}) copy-start(s32[8]{0:T(128)} %counts_ref.3) | copy-start | bytes 100
  14.3 11.9 %collective-permute-start.3 = (bf16[2,384,128]{2,1,0:T(8,128)(2,1)S(1)}, bf16[2,384,128]{2,1,0:T(8,128)(2,1)S(1)}, u32[]{:S(2)}, u32[]{:S(2)}) collective-permute-start(bf16[2,384,128]{2,1,0:T(8,128)(2,1)S(1)} %get-tuple-element.30), channel_id=1, source_target_pairs={{0,24},{4,28},{8,16},{12,20},{16,8},{20,12},{24,0},{28,4},{1,25},{... | collective-permute-start | bytes 589832 | tf_op jit(solution)/shard_map/ppermute | solution.py:441
  37.1 34.1 %collective-permute-start.14 = (bf16[4,256,128]{2,1,0:T(8,128)(2,1)S(1)}, bf16[4,256,128]{2,1,0:T(8,128)(2,1)S(1)}, u32[]{:S(2)}, u32[]{:S(2)}) collective-permute-start(bf16[4,256,128]{2,1,0:T(8,128)(2,1)S(1)} %get-tuple-element.44), channel_id=1, source_target_pairs={{0,4},{4,0},{8,12},{12,8},{16,20},{20,16},{24,28},{28,24},{1,5},{5... | collective-permute-start | bytes 786440 | tf_op jit(solution)/shard_map/ppermute | solution.py:428
  37.7 1.2 %collective-permute-start.11 = (f32[1,128]{1,0:T(1,128)S(1)}, f32[1,128]{1,0:T(1,128)S(1)}, u32[]{:S(2)}, u32[]{:S(2)}) collective-permute-start(f32[1,128]{1,0:T(1,128)S(1)} %get-tuple-element.42), channel_id=1, source_target_pairs={{0,4},{4,0},{8,12},{12,8},{16,20},{20,16},{24,28},{28,24},{1,5},{5... | collective-permute-start | bytes 1544 | tf_op jit(solution)/shard_map/ppermute | solution.py:529
  38.9 3.6 %collective-permute-start.12 = (f32[1,128]{1,0:T(1,128)S(1)}, f32[1,128]{1,0:T(1,128)S(1)}, u32[]{:S(2)}, u32[]{:S(2)}) collective-permute-start(f32[1,128]{1,0:T(1,128)S(1)} %add.6), channel_id=1, source_target_pairs={{0,1},{1,0},{2,3},{3,2},{4,5},{5,4},{6,7},{7,6},{8,9},{9,8},{10,11... | collective-permute-start | bytes 1544 | tf_op jit(solution)/shard_map/ppermute | solution.py:534
  42.5 28.7 %collective-permute-start.13 = (f32[1,128]{1,0:T(1,128)S(1)}, f32[1,128]{1,0:T(1,128)S(1)}, u32[]{:S(2)}, u32[]{:S(2)}) collective-permute-start(f32[1,128]{1,0:T(1,128)S(1)} %add.7.refs_0_), channel_id=1, source_target_pairs={{0,2},{1,3},{2,0},{3,1},{4,6},{5,7},{6,4},{7,5},{8,10},{9,11},{10,... | collective-permute-start | bytes 1544 | tf_op jit(solution)/shard_map/ppermute | solution.py:534
  71.2 5.6 %collective-permute-start.15 = (bf16[2,272,128]{2,1,0:T(8,128)(2,1)S(1)}, bf16[2,272,128]{2,1,0:T(8,128)(2,1)S(1)}, u32[]{:S(2)}, u32[]{:S(2)}) collective-permute-start(bf16[2,272,128]{2,1,0:T(8,128)(2,1)S(1)} %get-tuple-element.45), channel_id=1, source_target_pairs={{0,8},{4,12},{8,0},{12,4},{16,24},{20,28},{24,16},{28,20},{1,9},{5... | collective-permute-start | bytes 417800 | tf_op jit(solution)/shard_map/ppermute | solution.py:441
  71.3 7.0 %collective-permute-start.16 = (bf16[2,272,128]{2,1,0:T(8,128)(2,1)S(1)}, bf16[2,272,128]{2,1,0:T(8,128)(2,1)S(1)}, u32[]{:S(2)}, u32[]{:S(2)}) collective-permute-start(bf16[2,272,128]{2,1,0:T(8,128)(2,1)S(1)} %get-tuple-element.46), channel_id=1, source_target_pairs={{0,16},{4,20},{8,24},{12,28},{16,0},{20,4},{24,8},{28,12},{1,17},{... | collective-permute-start | bytes 417800 | tf_op jit(solution)/shard_map/ppermute | solution.py:441
  71.4 6.9 %collective-permute-start.17 = (bf16[2,272,128]{2,1,0:T(8,128)(2,1)S(1)}, bf16[2,272,128]{2,1,0:T(8,128)(2,1)S(1)}, u32[]{:S(2)}, u32[]{:S(2)}) collective-permute-start(bf16[2,272,128]{2,1,0:T(8,128)(2,1)S(1)} %get-tuple-element.47), channel_id=1, source_target_pairs={{0,24},{4,28},{8,16},{12,20},{16,8},{20,12},{24,0},{28,4},{1,25},{... | collective-permute-start | bytes 417800 | tf_op jit(solution)/shard_map/ppermute | solution.py:441
